TPU v7x, 256 devices: a whole 4x4x8 slice. The times are simulated.
256 devices in a mesh: rows: 32 (over x, y, core), snaps: 8 (over z).
Axes of the slice: x: 4, y: 4, z: 8, core: 2. Of those that a mesh axis runs over, the one named last changes fastest.
Arguments:
- snapshots: bfloat16 [262144, 4096], P('rows', 'snaps'), may hold values from -22 to 22
- sketch: bfloat16 [4096, 128], P('snaps'), may hold values from -0.09375 to 0.09375
Outputs:
- basis: float32 [262144, 128], P(('rows', 'snaps'))
- projected: float32 [128, 4096], P('rows', 'snaps')
All inputs are finite; a program needn't handle non-finite values.
Results may differ from a plain program's by a relative error of at most 0.00055.
Values may be sent and summed in bfloat16 or wider, within the bound.
A program may use at most 64 MiB of HBM per device.

v0:
```python
import math

import jax
import jax.numpy as jnp
from jax import lax
from jax.sharding import PartitionSpec as P


def gram_part(sampled):
    return jnp.dot(sampled.T, sampled, precision=lax.Precision.HIGHEST)


def solve_rows(lower, sampled):
    return lax.linalg.triangular_solve(
        lower, sampled, left_side=False, lower=True, transpose_a=True
    )


def local(snapshots, sketch):
    total = snapshots.shape[0] * lax.axis_size("rows")
    partial_value = jnp.dot(snapshots, sketch, preferred_element_type=jnp.float32)
    sampled = lax.psum(partial_value, "snaps")
    gram = lax.psum(gram_part(sampled), "rows") / total
    lower = jnp.linalg.cholesky(gram)
    full_basis = solve_rows(lower, sampled)
    share = full_basis.shape[0] // lax.axis_size("snaps")
    basis = lax.dynamic_slice_in_dim(full_basis, lax.axis_index("snaps") * share, share, 0)
    coarse = full_basis.astype(jnp.bfloat16)
    factor = 1.0 / math.sqrt(total)
    owned = coarse.shape[1] // lax.axis_size("rows")
    summed = lax.psum(
        jnp.einsum("mk,mn->kn", coarse, snapshots, preferred_element_type=jnp.float32) * factor,
        "rows",
    )
    projected = lax.dynamic_slice_in_dim(summed, lax.axis_index("rows") * owned, owned, 0)
    return (basis, projected)


def solution(mesh):
    in_specs = (P("rows", "snaps"), P("snaps", None))
    out_specs = (P(("rows", "snaps"), None), P("rows", "snaps"))
    return jax.shard_map(local, mesh=mesh, in_specs=in_specs, out_specs=out_specs, check_vma=False)
```

profile of v0, /device:TPU:1, one launch (start us, length us, event | category | flops | bytes accessed | tf_op | source)
XLA Modules:
  0.0 399.7 jit_solution(17600114579511021193)
XLA Ops:
  7.2 0.0 copy-start
  7.2 0.0 all-reduce.4.cloned.1.call-start
  7.2 0.8 copy-done
  8.1 7.7 %fusion.9 = f32[8192,128]{1,0:T(8,128)} fusion(bf16[8192,512]{1,0:T(8,128)(2,1)} %param.2, bf16[512,128]{1,0:T(8,128)(2,1)S(1)} %copy-done), kind=kOutput, calls=%fused_computation.16 | convolution fusion | flops 1073741824 | bytes 12713984 | tf_op jit(solution)/shard_map/dot_general | solution.py:21
  15.8 0.0 all-reduce.4.cloned.1.call-update
  15.8 0.0 all-reduce.6.cloned.1.call-start
  15.8 112.9 %all-reduce.4.cloned.1.call-done = f32[8192,128]{1,0:T(8,128)} async-done(((f32[8192,128]{1,0:T(8,128)}), f32[8192,128]{1,0:T(8,128)}) %all-reduce.4.cloned.1.call-update) | async-done | bytes 4194320 | tf_op jit(solution)/shard_map/psum | solution.py:22
  128.7 10.8 %fusion.10 = f32[128,128]{0,1:T(8,128)} fusion(f32[8192,128]{1,0:T(8,128)} %all-reduce.4.cloned.1.call-done), kind=kOutput, calls=%fused_computation.17 | convolution fusion | flops 1610612736 | bytes 4259840 | tf_op jit(solution)/shard_map/dot_general | solution.py:10
  139.6 0.0 all-reduce.6.cloned.1.call-update
  139.6 0.2 all-reduce.8.cloned.1.call-start
  139.8 104.6 %all-reduce.6.cloned.1.call-done = f32[128,128]{0,1:T(8,128)} async-done(((f32[128,128]{0,1:T(8,128)}), f32[128,128]{0,1:T(8,128)}) %all-reduce.6.cloned.1.call-update) | async-done | bytes 65552 | tf_op jit(solution)/shard_map/psum | solution.py:23
  244.4 0.8 broadcast_multiply_fusion
  245.3 0.1 copy.5
  245.4 0.9 fusion.8
  246.2 11.7 %cholesky.16 = f32[128,128]{1,0:T(8,128)S(1)} custom-call(f32[128,128]{1,0:T(8,128)S(1)} %fusion.8), custom_call_target="Cholesky" | custom-call | tf_op jit(solution)/shard_map/jit(cholesky)/cholesky | solution.py:24
  258.0 0.6 compare_reduce_fusion
  258.6 0.7 fusion.5
  259.3 9.8 %custom-call.6 = f32[1,128,128]{1,2,0:T(8,128)S(1)} custom-call(f32[1,128,128]{2,1,0:T(8,128)S(1)} %fusion.5), custom_call_target="InvertDiagBlocksLowerTriangular" | custom-call | tf_op jit(solution)/shard_map/triangular_solve | solution.py:14
  269.1 5.2 %fusion.6 = f32[8192,128]{1,0:T(8,128)S(1)} fusion(f32[8192,128]{1,0:T(8,128)} %all-reduce.4.cloned.1.call-done, f32[1,128,128]{1,2,0:T(8,128)S(1)} %custom-call.6), kind=kOutput, calls=%fused_computation.5 | convolution fusion | flops 1610612736 | bytes 8454144 | tf_op jit(solution)/shard_map/triangular_solve | solution.py:14
  274.3 0.0 copy-start.1
  274.3 1.9 copy-done.1
  276.2 5.4 %fusion.2 = f32[128,512]{1,0:T(8,128)} fusion(bf16[8192,512]{1,0:T(8,128)(2,1)} %param.2, f32[8192,128]{1,0:T(8,128)S(1)} %fusion.6), kind=kOutput, calls=%fused_computation.2 | convolution fusion | flops 1074855936 | bytes 12845056 | tf_op jit(solution)/shard_map/mk,mn->kn/dot_general | solution.py:32
  281.6 0.0 all-reduce.8.cloned.1.call-update
  281.6 1.9 constant_dynamic-slice_fusion.1
  283.5 108.3 %all-reduce.8.cloned.1.call-done = f32[128,512]{1,0:T(8,128)} async-done(((f32[128,512]{1,0:T(8,128)}), f32[128,512]{1,0:T(8,128)}) %all-reduce.8.cloned.1.call-update) | async-done | bytes 262160 | tf_op jit(solution)/shard_map/psum | solution.py:31
  391.8 1.3 constant_dynamic-slice_fusion
  (1 shorter events, 0.0 us)
Async XLA Ops:
  7.2 0.9 copy-start
  7.2 121.6 %all-reduce.4.cloned.1.call-start = ((), (), s32[]{:S(2)}) async-start(), calls=%async_computation | async-start | bytes 8388608 | tf_op jit(solution)/shard_map/psum | solution.py:22
  15.8 228.6 %all-reduce.6.cloned.1.call-start = ((), (), s32[]{:S(2)}) async-start(), calls=%async_computation.1 | async-start | bytes 131072 | tf_op jit(solution)/shard_map/psum | solution.py:23
  139.6 252.2 %all-reduce.8.cloned.1.call-start = ((), (), s32[]{:S(2)}) async-start(), calls=%async_computation.2 | async-start | bytes 524288 | tf_op jit(solution)/shard_map/psum | solution.py:31
  274.3 1.9 copy-start.1
Sparse Core Ops, SparseCore 0:
  15.9 112.7 all-reduce.3
  139.7 104.6 all-reduce.5
  281.7 110.0 all-reduce.7
where the time goes:
time: 400 us
  waiting for transfers between devices  326 us (82%)
  matrix products  29.1 us (7%)
  other arithmetic  24.6 us (6%)
  between operations  13.8 us (3%)
  local copies, waits for them, and re-layouts  6.05 us (2%)
    psum x1, waiting for transfers between devices, local(): sampled = lax.psum(partial_value, 'snaps')  113 us
    psum x1, waiting for transfers between devices, local(): lax.psum(jnp.einsum('mk,mn->kn', coarse, snapshots, preferred_element_typ...  108 us
    psum x1, waiting for transfers between devices, local(): gram = lax.psum(gram_part(sampled), 'rows') / total  105 us
    another operation x3, other arithmetic, local(): lower = jnp.linalg.cholesky(gram)  12.4 us
    dot_general x1, matrix products, gram_part(): return jnp.dot(sampled.T, sampled, precision=lax.Precision.HIGHEST)  10.8 us
    another operation x2, other arithmetic, solve_rows(): lax.linalg.triangular_solve(lower, sampled, left_side=False, lower=True,...  10.5 us
  transfers between devices with their start and end apart: 3, of which 3 were waited for; matrix products, arithmetic and copies ran while one was open for 0% of the time, Pallas kernels for 0%

commit v1 on v0

v1 whole, which is shorter than its diff:
```python
import functools
import math

import jax
import jax.numpy as jnp
from jax import lax
from jax.experimental import pallas as pl
from jax.experimental.pallas import tpu as pltpu
from jax.sharding import PartitionSpec as P

MESH = pl.DeviceIdType.MESH
HIGHEST = lax.Precision.HIGHEST
F32, BF16 = jnp.float32, jnp.bfloat16

RING = 8
PIECES = 4
EVENTS = 2 * (RING - 1)
SPAN = 120.0
BLOCK = 16


def encode(value, buf):
    rows, rank = value.shape
    groups = value.reshape(rows // 16, 16, rank)
    size = jnp.abs(groups)
    top = (jnp.max(size, axis=0) * 1.01 + 1e-30).astype(BF16)
    buf[rows : rows + 16, :] = top
    gain = (2.0 * SPAN) / top.astype(F32)
    code = jnp.exp2(size * gain[None] - SPAN)
    code = jnp.where(groups < 0.0, -code, code)
    buf[0:rows, :] = code.reshape(rows, rank).astype(BF16)


def decode(buf):
    rows, rank = buf.shape[0] - 16, buf.shape[1]
    code = buf[0:rows, :].astype(F32).reshape(rows // 16, 16, rank)
    top = buf[rows : rows + 16, :].astype(F32)
    gain = top * (1.0 / (2.0 * SPAN * math.log(2.0)))
    size = (jnp.log(jnp.abs(code)) + SPAN * math.log(2.0)) * gain[None]
    return jnp.where(code < 0.0, -size, size).reshape(rows, rank)


def split(value):
    high = value.astype(BF16)
    return high, (value - high.astype(F32)).astype(BF16)


def factor_block(x, block):
    rank = x.shape[0]
    first = pl.multiple_of(block * BLOCK, BLOCK)
    shape = (BLOCK, rank)
    panel = x[pl.ds(first, BLOCK), :]
    left, right = panel[:, :rank], panel[:, rank:]
    corner = pltpu.roll(left, lax.rem(rank - first, rank), 1)
    row = lax.broadcasted_iota(jnp.int32, shape, 0)
    lane = lax.broadcasted_iota(jnp.int32, shape, 1)
    columns = [jnp.broadcast_to(corner[:, j : j + 1], shape) for j in range(BLOCK)]

    def spread(value, i):
        return jnp.broadcast_to(value[i : i + 1, :], shape)

    first_pivot = cross = determinant = jnp.zeros(shape, F32)
    for i in range(0, BLOCK, 2):
        one, two = columns[i], columns[i + 1]
        a, b, d = spread(one, i), spread(one, i + 1), spread(two, i + 1)
        det = a * d - b * b
        here = (row == i) | (row == i + 1)
        first_pivot = jnp.where(here, a, first_pivot)
        cross = jnp.where(row == i + 1, b, cross)
        determinant = jnp.where(here, det, determinant)
        if i + 2 == BLOCK:
            break
        inverse = jnp.where(row > i + 1, 1.0 / det, 0.0)
        u, v = (one * d - two * b) * inverse, (two * a - one * b) * inverse
        for j in range(i + 2, BLOCK):
            columns[j] = columns[j] - (u * spread(columns[j], i) + v * spread(columns[j], i + 1))
        left = left - (u * spread(left, i) + v * spread(left, i + 1))
        right = right - (u * spread(right, i) + v * spread(right, i + 1))
    odd = row % 2 == 1
    factor = cross / first_pivot
    scale = jnp.where(odd, first_pivot * lax.rsqrt(first_pivot * determinant), lax.rsqrt(first_pivot))
    left = (left - factor * pltpu.roll(left, 1, 0)) * scale
    right = (right - factor * pltpu.roll(right, 1, 0)) * scale
    whole = jnp.concatenate([left, right], axis=1)
    x[pl.ds(first, BLOCK), :] = whole
    r1, r2 = split(whole)
    r3 = (whole - r1.astype(F32) - r2.astype(F32)).astype(BF16)
    later = jnp.where(lane >= first + BLOCK, left, 0.0)
    l1, l2 = split(later)
    l3 = (later - l1.astype(F32) - l2.astype(F32)).astype(BF16)
    x[...] -= lax.dot_general(
        jnp.concatenate([l1, l1, l2, l1, l2, l3], axis=0),
        jnp.concatenate([r1, r2, r1, r3, r2, r1], axis=0),
        (((0,), (0,)), ((), ())),
        preferred_element_type=F32,
    )


def kernel(
    total, s_hbm, k_hbm, basis_hbm, proj_ref,
    s, k, part, tx, rx, everyone, z_sum, gg, g, g1, g2, g3, x, give, take, pair, zr, white,
    load_sem, rs_send, rs_recv, ag_send, ag_recv, g1_send, g1_recv, g2_send, g2_recv, g3_send, g3_recv,
    zr_send, zr_recv, mate_send, mate_recv, out_sem,
):
    chips = lax.axis_size("rows") // 2
    r, z = lax.axis_index("rows"), lax.axis_index("snaps")
    chip, core = lax.div(r, 2), lax.rem(r, 2)
    spot = z * 2 + core
    shard = part.shape[1]
    size = shard // PIECES
    rank = k.shape[1]
    own = rank // chips

    def at(step):
        return lax.rem(z + step + RING, RING)

    def load(offset, slot):
        rows = pl.ds(pl.multiple_of(at(offset) * shard, shard), shard)
        return pltpu.make_async_copy(s_hbm.at[rows, :], s.at[rows, :], load_sem.at[slot])

    order = (4, 3, -3, 2, -2, 1, -1, 0)
    sketch_copy = pltpu.make_async_copy(k_hbm, k, load_sem.at[RING])
    sketch_copy.start()
    for slot, offset in enumerate(order):
        load(offset, slot).start()

    barrier = pltpu.get_barrier_semaphore()

    def other_chip(step):
        return lax.rem(chip + step, chips)

    def other_spot(step):
        return lax.rem(spot + step, 2 * RING)

    def to_chip(step):
        return {"rows": other_chip(step) * 2 + core, "snaps": z}

    def to_spot(step):
        there = other_spot(step)
        return {"rows": chip * 2 + lax.rem(there, 2), "snaps": lax.div(there, 2)}

    @pl.loop(1, chips)
    def _(step):
        pl.semaphore_signal(barrier, inc=1, device_id=to_chip(step), device_id_type=MESH)

    @pl.loop(1, 2 * RING)
    def _(step):
        pl.semaphore_signal(barrier, inc=1, device_id=to_spot(step), device_id_type=MESH)

    def ring(side, src, dst, send, recv):
        return pltpu.make_async_remote_copy(
            src_ref=src,
            dst_ref=dst,
            send_sem=send,
            recv_sem=recv,
            device_id={"rows": r, "snaps": at(1 - 2 * side)},
            device_id_type=MESH,
        )

    def sum_copy(side, t):
        return ring(side, tx.at[side, t], rx.at[side, t], rs_send.at[side, t], rs_recv.at[side, t])

    def piece(q):
        return pl.ds(pl.multiple_of(q * size, size), size)

    def sketch(offset, slot):
        load(offset, slot).wait()
        j = at(offset)

        @pl.loop(0, PIECES)
        def _(q):
            rows = pl.ds(pl.multiple_of(j * shard + q * size, size), size)
            part[j, piece(q), :] = jnp.dot(s[rows, :], k[...], preferred_element_type=F32)

    def head(side, t, offset, q):
        encode(part[at(offset), piece(q), :], tx.at[side, t])
        sum_copy(side, t).start()

    sketch_copy.wait()
    sketch(order[0], 0)
    pl.semaphore_wait(barrier, chips - 1 + 2 * RING - 1)

    @pl.loop(0, 2)
    def _(i):
        head(0, i, 4, i)
        head(1, i, 4, 2 + i)

    sketch(order[1], 1)

    @pl.loop(0, 2)
    def _(i):
        head(0, 2 + i, 3, 2 + i)

    sketch(order[2], 2)

    @pl.loop(0, 2)
    def _(i):
        head(1, 2 + i, -3, i)

    for slot in range(3, RING):
        sketch(order[slot], slot)

    def turn(side, t):
        pair, i = t // 2, t % 2
        odd = pair % 2
        far = 4 - (pair + 1) // 2
        return far, i + 2 * (odd if side == 0 else 1 - odd)

    @pl.loop(0, EVENTS - 4)
    def _(t):
        for side in range(2):
            far, q = turn(side, t)
            j = at((1 - 2 * side) * (far - 1))
            sum_copy(side, t).wait_recv()
            encode(part[j, piece(q), :] + decode(rx.at[side, t]), tx.at[side, t + 4])
            sum_copy(side, t + 4).start()

    def gather_copy(side, e, j, q):
        block = everyone.at[j, piece(q), :]
        return ring(side, block, block, ag_send.at[side, e], ag_recv.at[side, e])

    def gather_piece(side, e):
        hop = jnp.minimum(e // 4 + 1, 4)
        i = jnp.where(e < 12, e % 4, 2 * (e - 12))
        odd = i % 2
        return hop, 2 * (odd if side == 0 else 1 - odd) + i // 2

    @pl.loop(EVENTS - 4, EVENTS - 2)
    def _(t):
        for side in range(2):
            _, q = turn(side, t)
            sum_copy(side, t).wait_recv()
            part[z, piece(q), :] += decode(rx.at[side, t])

    def gram(q):
        both = jnp.concatenate(split(part[z, piece(q), :]), axis=1)
        gg[...] += lax.dot_general(both, both, (((0,), (0,)), ((), ())), preferred_element_type=F32)

    gg[...] = jnp.zeros_like(gg)

    @pl.loop(EVENTS - 2, EVENTS)
    def _(t):
        for side in range(2):
            _, q = turn(side, t)
            sum_copy(side, t).wait_recv()
            mine = part[z, piece(q), :] + decode(rx.at[side, t])
            part[z, piece(q), :] = mine
            everyone[z, piece(q), :] = mine.astype(BF16)
        for side in range(2):
            for odd in range(2):
                e = 2 * (t - (EVENTS - 2)) + odd
                gather_copy(side, e, z, gather_piece(side, e)[1]).start()

        for side in range(2):
            gram(turn(side, t)[1])

    g[...] = gg[:rank, :rank] + gg[:rank, rank:] + gg[rank:, :rank] + gg[rank:, rank:]

    def block_of(index):
        return pl.ds(pl.multiple_of(index * own, own), own)

    def plane_copy(step, src, dst, send, recv, slot):
        return pltpu.make_async_remote_copy(
            src_ref=src,
            dst_ref=dst,
            send_sem=send.at[step],
            recv_sem=recv.at[slot],
            device_id=to_chip(step),
            device_id_type=MESH,
        )

    def g1_copy(step, slot):
        return plane_copy(step, g.at[block_of(other_chip(step)), :], g1.at[slot], g1_send, g1_recv, slot)

    def g2_copy(step, slot):
        return pltpu.make_async_remote_copy(
            src_ref=g2.at[spot],
            dst_ref=g2.at[slot],
            send_sem=g2_send.at[step],
            recv_sem=g2_recv.at[slot],
            device_id=to_spot(step),
            device_id_type=MESH,
        )

    def g3_copy(step, slot):
        return plane_copy(step, g3.at[block_of(chip), :], g3.at[block_of(slot), :], g3_send, g3_recv, slot)

    def zr_copy(step, slot):
        return plane_copy(step, pair.at[other_chip(step)], zr.at[slot], zr_send, zr_recv, slot)

    @pl.loop(1, chips)
    def _(step):
        g1_copy(step, chip).start()

    z_sum[...] = jnp.zeros_like(z_sum)

    def project(j, q):
        rows = pl.ds(pl.multiple_of(j * shard + q * size, size), size)
        z_sum[...] += lax.dot_general(
            everyone[j, piece(q), :], s[rows, :], (((0,), (0,)), ((), ())), preferred_element_type=F32
        )

    def gather(e):
        for side in range(2):
            hop, q = gather_piece(side, e)
            j = at(-(1 - 2 * side) * hop)
            gather_copy(side, e, j, q).wait_recv()

            @pl.when((e < 8) | (e == 8) | (e == 10))
            def _():
                gather_copy(side, jnp.where(e < 8, e + 4, 12 + (e - 8) // 2), j, q).start()

        for side in range(2):
            hop, q = gather_piece(side, e)
            project(at(-(1 - 2 * side) * hop), q)

    @pl.loop(0, PIECES)
    def _(q):
        project(z, q)

    gather(0)

    @pl.loop(1, chips)
    def _(step):
        g1_copy(step, other_chip(step)).wait_recv()

    g1[chip] = g[block_of(chip), :]
    g2[spot] = jnp.sum(g1[...], axis=0)

    @pl.loop(1, 2 * RING)
    def _(step):
        g2_copy(step, spot).start()

    @pl.loop(1, 3)
    def _(e):
        gather(e)

    @pl.loop(1, 2 * RING)
    def _(step):
        g2_copy(step, other_spot(step)).wait_recv()

    g3[block_of(chip), :] = jnp.sum(g2[...], axis=0) * (1.0 / total)

    @pl.loop(1, chips)
    def _(step):
        g3_copy(step, chip).start()

    @pl.loop(3, 5)
    def _(e):
        gather(e)

    @pl.loop(1, chips)
    def _(step):
        g3_copy(step, other_chip(step)).wait_recv()

    eye = lax.broadcasted_iota(jnp.int32, (rank, rank), 0) == lax.broadcasted_iota(jnp.int32, (rank, rank), 1)
    full = g3[...]
    diagonal = jnp.where(eye, full, 0.0)
    down = lax.rsqrt(jnp.sum(diagonal, axis=1, keepdims=True))
    across = lax.rsqrt(jnp.sum(diagonal, axis=0, keepdims=True))
    x[...] = jnp.concatenate([full * down * across, jnp.where(eye, down, 0.0)], axis=1)

    @pl.loop(5, EVENTS - 1)
    def _(e):
        gather(e)
        factor_block(x, e - 5)

    gather(EVENTS - 1)

    l1, l2 = split(x[:, rank:])
    z1, z2 = split(z_sum[...])
    term = jnp.dot(
        jnp.concatenate([l1, l2, l1], axis=1),
        jnp.concatenate([z1, z1, z2], axis=0),
        preferred_element_type=F32,
    ) * (1.0 / math.sqrt(total))
    half = own // 2
    z_sum[...] = term
    for c in range(chips):
        rows = z_sum[c * own : (c + 1) * own, :]
        low, high = rows[:half], rows[half:]
        give[c] = jnp.where(core == 0, high, low)
        pair[c] = jnp.where(core == 0, low, high)
    mate = pltpu.make_async_remote_copy(
        src_ref=give,
        dst_ref=take,
        send_sem=mate_send,
        recv_sem=mate_recv,
        device_id={"rows": chip * 2 + 1 - core, "snaps": z},
        device_id_type=MESH,
    )
    mate.start()
    i1, i2 = split(x[:, rank:])
    mate.wait_recv()
    pair[...] += take[...]

    @pl.loop(1, chips)
    def _(step):
        zr_copy(step, chip).start()

    def basis_copy(q):
        return pltpu.make_async_copy(white.at[piece(q), :], basis_hbm.at[piece(q), :], out_sem.at[q])

    @pl.loop(0, PIECES)
    def _(q):
        y1, y2 = split(part[z, piece(q), :])
        white[piece(q), :] = lax.dot_general(
            jnp.concatenate([y1, y1, y2], axis=1),
            jnp.concatenate([i1, i2, i1], axis=1),
            (((1,), (1,)), ((), ())),
            preferred_element_type=F32,
        )
        basis_copy(q).start()

    @pl.loop(1, chips)
    def _(step):
        zr_copy(step, other_chip(step)).wait_recv()

    zr[chip] = pair[chip]
    proj_ref[...] = jnp.sum(zr[...], axis=0)

    @pl.loop(0, EVENTS)
    def _(t):
        for side in range(2):
            sum_copy(side, t).wait_send()
            gather_copy(side, t, z, 0).wait_send()

    @pl.loop(1, chips)
    def _(step):
        g1_copy(step, chip).wait_send()
        g3_copy(step, chip).wait_send()
        zr_copy(step, chip).wait_send()

    @pl.loop(1, 2 * RING)
    def _(step):
        g2_copy(step, spot).wait_send()

    @pl.loop(0, PIECES)
    def _(q):
        basis_copy(q).wait()

    mate.wait_send()


def finish(basis_in, proj_in, basis_out, proj_out, sem):
    copies = [pltpu.make_async_copy(proj_in, proj_out, sem.at[0])]
    size = basis_in.shape[0] // 4
    for q in range(4):
        rows = pl.ds(q * size, size)
        copies.append(pltpu.make_async_copy(basis_in.at[rows, :], basis_out.at[rows, :], sem.at[1 + q]))
    for copy in copies:
        copy.start()
    for copy in copies:
        copy.wait()


def local(snapshots, sketch):
    rows, columns = snapshots.shape
    rank = sketch.shape[1]
    chips = lax.axis_size("rows") // 2
    total = rows * lax.axis_size("rows")
    shard = rows // RING
    own = rank // chips
    message = shard // PIECES + 16
    dma = pltpu.SemaphoreType.DMA
    outputs = (
        jax.ShapeDtypeStruct((shard, rank), F32),
        jax.ShapeDtypeStruct((own // 2, columns), F32),
    )
    anywhere = pl.BlockSpec(memory_space=pl.ANY)
    basis, projected = pl.pallas_call(
        functools.partial(kernel, total),
        out_shape=outputs,
        in_specs=[anywhere] * 2,
        out_specs=(anywhere, pl.BlockSpec(memory_space=pltpu.VMEM)),
        scratch_shapes=[
            pltpu.VMEM((rows, columns), BF16),
            pltpu.VMEM((columns, rank), BF16),
            pltpu.VMEM((RING, shard, rank), F32),
            pltpu.VMEM((2, EVENTS, message, rank), BF16),
            pltpu.VMEM((2, EVENTS, message, rank), BF16),
            pltpu.VMEM((RING, shard, rank), BF16),
            pltpu.VMEM((rank, columns), F32),
            pltpu.VMEM((2 * rank, 2 * rank), F32),
            pltpu.VMEM((rank, rank), F32),
            pltpu.VMEM((chips, own, rank), F32),
            pltpu.VMEM((2 * RING, own, rank), F32),
            pltpu.VMEM((rank, rank), F32),
            pltpu.VMEM((rank, 2 * rank), F32),
            pltpu.VMEM((chips, own // 2, columns), F32),
            pltpu.VMEM((chips, own // 2, columns), F32),
            pltpu.VMEM((chips, own // 2, columns), F32),
            pltpu.VMEM((chips, own // 2, columns), F32),
            pltpu.VMEM((shard, rank), F32),
            dma((RING + 1,)),
            dma((2, EVENTS)),
            dma((2, EVENTS)),
            dma((2, EVENTS)),
            dma((2, EVENTS)),
            dma((chips,)),
            dma((chips,)),
            dma((2 * RING,)),
            dma((2 * RING,)),
            dma((chips,)),
            dma((chips,)),
            dma((chips,)),
            dma((chips,)),
            dma,
            dma,
            dma((PIECES,)),
        ],
        compiler_params=pltpu.CompilerParams(
            collective_id=0, has_side_effects=True, vmem_limit_bytes=56 * 1024 * 1024
        ),
    )(snapshots, sketch)
    return pl.pallas_call(
        finish,
        out_shape=outputs,
        in_specs=[anywhere] * 2,
        out_specs=(anywhere, anywhere),
        scratch_shapes=[dma((5,))],
        compiler_params=pltpu.CompilerParams(vmem_limit_bytes=63 * 1024 * 1024),
    )(basis, projected)


def solution(mesh):
    in_specs = (P("rows", "snaps"), P("snaps", None))
    out_specs = (P(("rows", "snaps"), None), P("rows", "snaps"))
    return jax.shard_map(local, mesh=mesh, in_specs=in_specs, out_specs=out_specs, check_vma=False)
```

time: 400 us -> 87.5 us (0.22)
  waiting for transfers between devices: 326 us -> 0 us
  Pallas kernels: 0 us -> 86.8 us
  matrix products: 29.1 us -> 0 us
  other arithmetic: 24.6 us -> 0 us
  between operations: 13.8 us -> 0.64 us
  local copies, waits for them, and re-layouts: 6.05 us -> 0 us
    psum x3 -> x0, waiting for transfers between devices: 326 us -> none  [the longest x1 113 us: local(): sampled = lax.psum(partial_value, 'snaps')]
    pallas_call x0 -> x2, Pallas kernels: none -> 86.8 us  [the longest x1 69.5 us: local(): pl.pallas_call(functools.partial(kernel, total), out_shape=outputs, in_sp...]
    dot_general x3 -> x0, matrix products: 23.9 us -> none  [the longest x1 10.8 us: gram_part(): return jnp.dot(sampled.T, sampled, precision=lax.Precision.HIGHEST)]
    another operation x5 -> x0, other arithmetic: 22.9 us -> none  [the longest x3 12.4 us: local(): lower = jnp.linalg.cholesky(gram)]
    another operation x1 -> x0, matrix products: 5.19 us -> none  [solve_rows(): lax.linalg.triangular_solve(lower, sampled, left_side=False, lower=True,...]
  transfers between devices with their start and end apart: 3 -> 0, of which waited for: 3 -> 0; matrix products, arithmetic and copies ran while one was open for 0% -> 0% of each run, Pallas kernels for 0% -> 0%
where the time goes in v1:
time: 87.5 us; the launch traced here: 87.4 us
  Pallas kernels  86.8 us (99%)
    pallas_call x1, Pallas kernels, local(): pl.pallas_call(functools.partial(kernel, total), out_shape=outputs, in_sp...  69.5 us
    pallas_call x1, Pallas kernels, local(): pl.pallas_call(finish, out_shape=outputs, in_specs=[anywhere] * 2, out_sp...  17.3 us

profile of v1, /device:TPU:1, one launch (start us, length us, event | category | flops | bytes accessed | tf_op | source)
XLA Modules:
  0.0 87.4 jit_solution(10119399654856498609)
XLA Ops:
  0.6 69.5 %shard_map.41 = (f32[1024,128]{1,0:T(8,128)}, f32[4,512]{1,0:T(4,128)}) custom-call(bf16[8192,512]{1,0:T(8,128)(2,1)} %s_hbm.1, bf16[512,128]{1,0:T(8,128)(2,1)} %k_hbm.1), custom_call_target="tpu_custom_call" | custom-call | tf_op jit(solution)/shard_map/pallas_call | solution.py:471
  70.2 17.3 %shard_map.42 = (f32[1024,128]{1,0:T(8,128)}, f32[4,512]{1,0:T(4,128)}) custom-call(f32[1024,128]{1,0:T(8,128)} %get-tuple-element.4.basis_in, f32[4,512]{1,0:T(4,128)} %get-tuple-element.5.proj_in), custom_call_target="tpu_custom_call" | custom-call | tf_op jit(solution)/shard_map/pallas_call | solution.py:516

commit v2 on v1

--- a/solution.py
+++ b/solution.py
@@ -22,22 +22,17 @@
 def encode(value, buf):
     rows, rank = value.shape
     groups = value.reshape(rows // 16, 16, rank)
-    size = jnp.abs(groups)
-    top = (jnp.max(size, axis=0) * 1.01 + 1e-30).astype(BF16)
+    top = (jnp.max(jnp.abs(groups), axis=0) * 1.01 + 1e-30).astype(BF16)
     buf[rows : rows + 16, :] = top
-    gain = (2.0 * SPAN) / top.astype(F32)
-    code = jnp.exp2(size * gain[None] - SPAN)
-    code = jnp.where(groups < 0.0, -code, code)
-    buf[0:rows, :] = code.reshape(rows, rank).astype(BF16)
+    gain = SPAN / top.astype(F32)
+    buf[0:rows, :] = jnp.exp2(groups * gain[None]).reshape(rows, rank).astype(BF16)
 
 
 def decode(buf):
     rows, rank = buf.shape[0] - 16, buf.shape[1]
     code = buf[0:rows, :].astype(F32).reshape(rows // 16, 16, rank)
-    top = buf[rows : rows + 16, :].astype(F32)
-    gain = top * (1.0 / (2.0 * SPAN * math.log(2.0)))
-    size = (jnp.log(jnp.abs(code)) + SPAN * math.log(2.0)) * gain[None]
-    return jnp.where(code < 0.0, -size, size).reshape(rows, rank)
+    gain = buf[rows : rows + 16, :].astype(F32) * (1.0 / (SPAN * math.log(2.0)))
+    return (jnp.log(code) * gain[None]).reshape(rows, rank)
 
 
 def split(value):
@@ -442,15 +437,18 @@
     mate.wait_send()
 
 
-def finish(basis_in, proj_in, basis_out, proj_out, sem):
-    copies = [pltpu.make_async_copy(proj_in, proj_out, sem.at[0])]
-    size = basis_in.shape[0] // 4
-    for q in range(4):
-        rows = pl.ds(q * size, size)
-        copies.append(pltpu.make_async_copy(basis_in.at[rows, :], basis_out.at[rows, :], sem.at[1 + q]))
-    for copy in copies:
+def finish(basis_in, proj_in, basis_out, proj_out, basis_held, proj_held, came, left):
+    size = basis_in.shape[0] // PIECES
+    rows = [pl.ds(q * size, size) for q in range(PIECES)]
+    trips = [(proj_in, proj_held, proj_out)] + [(basis_in.at[q], basis_held.at[q], basis_out.at[q]) for q in rows]
+    first = [pltpu.make_async_copy(a, b, came.at[i]) for i, (a, b, _) in enumerate(trips)]
+    second = [pltpu.make_async_copy(b, c, left.at[i]) for i, (_, b, c) in enumerate(trips)]
+    for copy in first:
         copy.start()
-    for copy in copies:
+    for came_in, copy in zip(first, second):
+        came_in.wait()
+        copy.start()
+    for copy in second:
         copy.wait()
 
 
@@ -518,7 +516,12 @@
         out_shape=outputs,
         in_specs=[anywhere] * 2,
         out_specs=(anywhere, anywhere),
-        scratch_shapes=[dma((5,))],
+        scratch_shapes=[
+            pltpu.VMEM(basis.shape, F32),
+            pltpu.VMEM(projected.shape, F32),
+            dma((PIECES + 1,)),
+            dma((PIECES + 1,)),
+        ],
         compiler_params=pltpu.CompilerParams(vmem_limit_bytes=63 * 1024 * 1024),
     )(basis, projected)
 

time: 87.5 us -> 72 us (0.82)
  Pallas kernels: 86.8 us -> 71.2 us
    pallas_call x1, Pallas kernels: 17.3 us -> 1.85 us  [local(): pl.pallas_call(finish, out_shape=outputs, in_specs=[anywhere] * 2, out_sp...]
where the time goes in v2:
time: 72 us; the launch traced here: 71.9 us
  Pallas kernels  71.2 us (99%)
    pallas_call x1, Pallas kernels, local(): pl.pallas_call(functools.partial(kernel, total), out_shape=outputs, in_sp...  69.4 us
    pallas_call x1, Pallas kernels, local(): pl.pallas_call(finish, out_shape=outputs, in_specs=[anywhere] * 2, out_sp...  1.85 us

profile of v2, /device:TPU:1, one launch (start us, length us, event | category | flops | bytes accessed | tf_op | source)
XLA Modules:
  0.0 71.9 jit_solution(1705315754402475755)
XLA Ops:
  0.6 69.4 %shard_map.41 = (f32[1024,128]{1,0:T(8,128)}, f32[4,512]{1,0:T(4,128)}) custom-call(bf16[8192,512]{1,0:T(8,128)(2,1)} %s_hbm.1, bf16[512,128]{1,0:T(8,128)(2,1)} %k_hbm.1), custom_call_target="tpu_custom_call" | custom-call | tf_op jit(solution)/shard_map/pallas_call | solution.py:469
  70.0 1.9 %shard_map.42 = (f32[1024,128]{1,0:T(8,128)}, f32[4,512]{1,0:T(4,128)}) custom-call(f32[1024,128]{1,0:T(8,128)} %get-tuple-element.4.basis_in, f32[4,512]{1,0:T(4,128)} %get-tuple-element.5.proj_in), custom_call_target="tpu_custom_call" | custom-call | tf_op jit(solution)/shard_map/pallas_call | solution.py:514

commit v3 on v2

--- a/solution.py
+++ b/solution.py
@@ -92,8 +92,8 @@
 
 
 def kernel(
-    total, s_hbm, k_hbm, basis_hbm, proj_ref,
-    s, k, part, tx, rx, everyone, z_sum, gg, g, g1, g2, g3, x, give, take, pair, zr, white,
+    total, s_hbm, k_hbm, basis_hbm, proj_hbm,
+    s, k, part, tx, rx, everyone, z_sum, gg, g, g1, g2, g3, x, give, take, pair, zr, white, shared,
     load_sem, rs_send, rs_recv, ag_send, ag_recv, g1_send, g1_recv, g2_send, g2_recv, g3_send, g3_recv,
     zr_send, zr_recv, mate_send, mate_recv, out_sem,
 ):
@@ -113,11 +113,13 @@
         rows = pl.ds(pl.multiple_of(at(offset) * shard, shard), shard)
         return pltpu.make_async_copy(s_hbm.at[rows, :], s.at[rows, :], load_sem.at[slot])
 
-    order = (4, 3, -3, 2, -2, 1, -1, 0)
+    def order(slot):
+        return (RING - slot) // 2 * (1 - 2 * ((slot + 1) % 2)) if slot else RING // 2
+
     sketch_copy = pltpu.make_async_copy(k_hbm, k, load_sem.at[RING])
     sketch_copy.start()
-    for slot, offset in enumerate(order):
-        load(offset, slot).start()
+    load(order(0), 0).start()
+    load(order(1), 1).start()
 
     barrier = pltpu.get_barrier_semaphore()
 
@@ -158,21 +160,20 @@
     def piece(q):
         return pl.ds(pl.multiple_of(q * size, size), size)
 
-    def sketch(offset, slot):
-        load(offset, slot).wait()
-        j = at(offset)
-
-        @pl.loop(0, PIECES)
-        def _(q):
-            rows = pl.ds(pl.multiple_of(j * shard + q * size, size), size)
-            part[j, piece(q), :] = jnp.dot(s[rows, :], k[...], preferred_element_type=F32)
+    def sketch(slot):
+        if slot + 2 < RING:
+            load(order(slot + 2), slot + 2).start()
+        load(order(slot), slot).wait()
+        j = at(order(slot))
+        rows = pl.ds(pl.multiple_of(j * shard, shard), shard)
+        part[j] = jnp.dot(s[rows, :], k[...], preferred_element_type=F32)
 
     def head(side, t, offset, q):
         encode(part[at(offset), piece(q), :], tx.at[side, t])
         sum_copy(side, t).start()
 
     sketch_copy.wait()
-    sketch(order[0], 0)
+    sketch(0)
     pl.semaphore_wait(barrier, chips - 1 + 2 * RING - 1)
 
     @pl.loop(0, 2)
@@ -180,20 +181,20 @@
         head(0, i, 4, i)
         head(1, i, 4, 2 + i)
 
-    sketch(order[1], 1)
+    sketch(1)
 
     @pl.loop(0, 2)
     def _(i):
         head(0, 2 + i, 3, 2 + i)
 
-    sketch(order[2], 2)
+    sketch(2)
 
     @pl.loop(0, 2)
     def _(i):
         head(1, 2 + i, -3, i)
 
     for slot in range(3, RING):
-        sketch(order[slot], slot)
+        sketch(slot)
 
     def turn(side, t):
         pair, i = t // 2, t % 2
@@ -227,8 +228,9 @@
             sum_copy(side, t).wait_recv()
             part[z, piece(q), :] += decode(rx.at[side, t])
 
-    def gram(q):
-        both = jnp.concatenate(split(part[z, piece(q), :]), axis=1)
+    def gram(pieces):
+        rows = jnp.concatenate([part[z, piece(q), :] for q in pieces], axis=0)
+        both = jnp.concatenate(split(rows), axis=1)
         gg[...] += lax.dot_general(both, both, (((0,), (0,)), ((), ())), preferred_element_type=F32)
 
     gg[...] = jnp.zeros_like(gg)
@@ -246,8 +248,7 @@
                 e = 2 * (t - (EVENTS - 2)) + odd
                 gather_copy(side, e, z, gather_piece(side, e)[1]).start()
 
-        for side in range(2):
-            gram(turn(side, t)[1])
+        gram([turn(side, t)[1] for side in range(2)])
 
     g[...] = gg[:rank, :rank] + gg[:rank, rank:] + gg[rank:, :rank] + gg[rank:, rank:]
 
@@ -287,32 +288,31 @@
     def _(step):
         g1_copy(step, chip).start()
 
-    z_sum[...] = jnp.zeros_like(z_sum)
-
-    def project(j, q):
-        rows = pl.ds(pl.multiple_of(j * shard + q * size, size), size)
-        z_sum[...] += lax.dot_general(
-            everyone[j, piece(q), :], s[rows, :], (((0,), (0,)), ((), ())), preferred_element_type=F32
+    def term_of(pairs):
+        left = [everyone[j, piece(q), :] for j, q in pairs]
+        right = [s[pl.ds(pl.multiple_of(j * shard + q * size, size), size), :] for j, q in pairs]
+        return lax.dot_general(
+            jnp.concatenate(left, axis=0),
+            jnp.concatenate(right, axis=0),
+            (((0,), (0,)), ((), ())),
+            preferred_element_type=F32,
         )
 
     def gather(e):
+        came = []
         for side in range(2):
             hop, q = gather_piece(side, e)
             j = at(-(1 - 2 * side) * hop)
+            came.append((j, q))
             gather_copy(side, e, j, q).wait_recv()
 
             @pl.when((e < 8) | (e == 8) | (e == 10))
             def _():
                 gather_copy(side, jnp.where(e < 8, e + 4, 12 + (e - 8) // 2), j, q).start()
 
-        for side in range(2):
-            hop, q = gather_piece(side, e)
-            project(at(-(1 - 2 * side) * hop), q)
-
-    @pl.loop(0, PIECES)
-    def _(q):
-        project(z, q)
-
+        z_sum[...] += term_of(came)
+
+    z_sum[...] = term_of([(z, q) for q in range(PIECES)])
     gather(0)
 
     @pl.loop(1, chips)
@@ -407,12 +407,7 @@
         )
         basis_copy(q).start()
 
-    @pl.loop(1, chips)
-    def _(step):
-        zr_copy(step, other_chip(step)).wait_recv()
-
-    zr[chip] = pair[chip]
-    proj_ref[...] = jnp.sum(zr[...], axis=0)
+    mate.wait_send()
 
     @pl.loop(0, EVENTS)
     def _(t):
@@ -424,17 +419,29 @@
     def _(step):
         g1_copy(step, chip).wait_send()
         g3_copy(step, chip).wait_send()
+
+    @pl.loop(1, 2 * RING)
+    def _(step):
+        g2_copy(step, spot).wait_send()
+
+    @pl.loop(1, chips)
+    def _(step):
+        zr_copy(step, other_chip(step)).wait_recv()
+
+    zr[chip] = pair[chip]
+    shared[...] = jnp.sum(zr[...], axis=0)
+    proj_copy = pltpu.make_async_copy(shared, proj_hbm, out_sem.at[PIECES])
+    proj_copy.start()
+
+    @pl.loop(1, chips)
+    def _(step):
         zr_copy(step, chip).wait_send()
-
-    @pl.loop(1, 2 * RING)
-    def _(step):
-        g2_copy(step, spot).wait_send()
 
     @pl.loop(0, PIECES)
     def _(q):
         basis_copy(q).wait()
 
-    mate.wait_send()
+    proj_copy.wait()
 
 
 def finish(basis_in, proj_in, basis_out, proj_out, basis_held, proj_held, came, left):
@@ -470,7 +477,7 @@
         functools.partial(kernel, total),
         out_shape=outputs,
         in_specs=[anywhere] * 2,
-        out_specs=(anywhere, pl.BlockSpec(memory_space=pltpu.VMEM)),
+        out_specs=(anywhere, anywhere),
         scratch_shapes=[
             pltpu.VMEM((rows, columns), BF16),
             pltpu.VMEM((columns, rank), BF16),
@@ -490,6 +497,7 @@
             pltpu.VMEM((chips, own // 2, columns), F32),
             pltpu.VMEM((chips, own // 2, columns), F32),
             pltpu.VMEM((shard, rank), F32),
+            pltpu.VMEM((own // 2, columns), F32),
             dma((RING + 1,)),
             dma((2, EVENTS)),
             dma((2, EVENTS)),
@@ -505,7 +513,7 @@
             dma((chips,)),
             dma,
             dma,
-            dma((PIECES,)),
+            dma((PIECES + 1,)),
         ],
         compiler_params=pltpu.CompilerParams(
             collective_id=0, has_side_effects=True, vmem_limit_bytes=56 * 1024 * 1024

time: 72 us -> 71.2 us (0.989)
  Pallas kernels: 71.2 us -> 70.4 us
    pallas_call x1, Pallas kernels: 69.4 us -> 68.5 us  [local(): pl.pallas_call(functools.partial(kernel, total), out_shape=outputs, in_sp...]
where the time goes in v3:
time: 71.2 us; the launch traced here: 71 us
  Pallas kernels  70.4 us (99%)
    pallas_call x1, Pallas kernels, local(): pl.pallas_call(functools.partial(kernel, total), out_shape=outputs, in_sp...  68.5 us
    pallas_call x1, Pallas kernels, local(): pl.pallas_call(finish, out_shape=outputs, in_specs=[anywhere] * 2, out_sp...  1.85 us

profile of v3, /device:TPU:1, one launch (start us, length us, event | category | flops | bytes accessed | tf_op | source)
XLA Modules:
  0.0 71.0 jit_solution(11752611256662348582)
XLA Ops:
  0.6 68.5 %shard_map.41 = (f32[1024,128]{1,0:T(8,128)}, f32[4,512]{1,0:T(4,128)}) custom-call(bf16[8192,512]{1,0:T(8,128)(2,1)} %s_hbm.1, bf16[512,128]{1,0:T(8,128)(2,1)} %k_hbm.1), custom_call_target="tpu_custom_call" | custom-call | tf_op jit(solution)/shard_map/pallas_call | solution.py:476
  69.2 1.9 %shard_map.42 = (f32[1024,128]{1,0:T(8,128)}, f32[4,512]{1,0:T(4,128)}) custom-call(f32[1024,128]{1,0:T(8,128)} %get-tuple-element.4.basis_in, f32[4,512]{1,0:T(4,128)} %get-tuple-element.5.proj_in), custom_call_target="tpu_custom_call" | custom-call | tf_op jit(solution)/shard_map/pallas_call | solution.py:522

commit v4 on v3

v4 whole, which is shorter than its diff:
```python
import functools
import math

import jax
import jax.numpy as jnp
from jax import lax
from jax.experimental import pallas as pl
from jax.experimental.pallas import tpu as pltpu
from jax.sharding import PartitionSpec as P

MESH = pl.DeviceIdType.MESH
HIGHEST = lax.Precision.HIGHEST
F32, BF16 = jnp.float32, jnp.bfloat16

RING = 8
PIECES = 4
EVENTS = 2 * (RING - 1)
SPAN = 120.0
BLOCK = 16


def groups_of(value):
    rows, rank = value.shape
    return value.reshape(rows // 16, 16, rank)


def peak(value):
    return jnp.max(jnp.abs(groups_of(value)), axis=0)


def encode(value, top):
    gain = SPAN / top.astype(F32)
    return jnp.exp2(groups_of(value) * gain[None]).reshape(value.shape).astype(BF16)


def decode(code, top):
    gain = top.astype(F32) * (1.0 / (SPAN * math.log(2.0)))
    return (jnp.log(groups_of(code.astype(F32))) * gain[None]).reshape(code.shape)


def split(value):
    high = value.astype(BF16)
    return high, (value - high.astype(F32)).astype(BF16)


def factor_block(x, block):
    rank = x.shape[0]
    first = pl.multiple_of(block * BLOCK, BLOCK)
    shape = (BLOCK, rank)
    panel = x[pl.ds(first, BLOCK), :]
    left, right = panel[:, :rank], panel[:, rank:]
    corner = pltpu.roll(left, lax.rem(rank - first, rank), 1)
    row = lax.broadcasted_iota(jnp.int32, shape, 0)
    lane = lax.broadcasted_iota(jnp.int32, shape, 1)
    columns = [jnp.broadcast_to(corner[:, j : j + 1], shape) for j in range(BLOCK)]

    def spread(value, i):
        return jnp.broadcast_to(value[i : i + 1, :], shape)

    first_pivot = cross = determinant = jnp.zeros(shape, F32)
    for i in range(0, BLOCK, 2):
        one, two = columns[i], columns[i + 1]
        a, b, d = spread(one, i), spread(one, i + 1), spread(two, i + 1)
        det = a * d - b * b
        here = (row == i) | (row == i + 1)
        first_pivot = jnp.where(here, a, first_pivot)
        cross = jnp.where(row == i + 1, b, cross)
        determinant = jnp.where(here, det, determinant)
        if i + 2 == BLOCK:
            break
        inverse = jnp.where(row > i + 1, 1.0 / det, 0.0)
        u, v = (one * d - two * b) * inverse, (two * a - one * b) * inverse
        for j in range(i + 2, BLOCK):
            columns[j] = columns[j] - (u * spread(columns[j], i) + v * spread(columns[j], i + 1))
        left = left - (u * spread(left, i) + v * spread(left, i + 1))
        right = right - (u * spread(right, i) + v * spread(right, i + 1))
    odd = row % 2 == 1
    factor = cross / first_pivot
    scale = jnp.where(odd, first_pivot * lax.rsqrt(first_pivot * determinant), lax.rsqrt(first_pivot))
    left = (left - factor * pltpu.roll(left, 1, 0)) * scale
    right = (right - factor * pltpu.roll(right, 1, 0)) * scale
    whole = jnp.concatenate([left, right], axis=1)
    x[pl.ds(first, BLOCK), :] = whole
    r1, r2 = split(whole)
    r3 = (whole - r1.astype(F32) - r2.astype(F32)).astype(BF16)
    later = jnp.where(lane >= first + BLOCK, left, 0.0)
    l1, l2 = split(later)
    l3 = (later - l1.astype(F32) - l2.astype(F32)).astype(BF16)
    x[...] -= lax.dot_general(
        jnp.concatenate([l1, l1, l2, l1, l2, l3], axis=0),
        jnp.concatenate([r1, r2, r1, r3, r2, r1], axis=0),
        (((0,), (0,)), ((), ())),
        preferred_element_type=F32,
    )


def kernel(
    total, s_hbm, k_hbm, basis_ref, proj_ref,
    s, k, part, tx, rx, everyone, z_sum, gg, g, g0, g1, g2, g3, x, give, take, pair, zr,
    load_sem, rs_send, rs_recv, ag_send, ag_recv, g1_sem, g2_sem, g3_sem, zr_sem, mate_send, mate_recv,
):
    count = lax.axis_size("rows")
    chips = count // 2
    r, z = lax.axis_index("rows"), lax.axis_index("snaps")
    chip, core = lax.div(r, 2), lax.rem(r, 2)
    shard = part.shape[1]
    size = shard // PIECES
    rank = k.shape[1]
    own = rank // chips
    half = rank // count

    def wrap(index, length):
        index = jnp.where(index >= length, index - length, index)
        return jnp.where(index < 0, index + length, index)

    def at(step):
        return wrap(z + step, RING)

    def load(offset, slot, part_of=0, parts=1):
        length = shard // parts
        rows = pl.ds(pl.multiple_of(at(offset) * shard + part_of * length, length), length)
        return pltpu.make_async_copy(s_hbm.at[rows, :], s.at[rows, :], load_sem.at[slot])

    def order(slot):
        return (RING - slot) // 2 * (1 - 2 * ((slot + 1) % 2)) if slot else RING // 2

    sketch_copy = pltpu.make_async_copy(k_hbm, k, load_sem.at[RING])
    sketch_copy.start()
    for side in range(2):
        load(order(0), side * (RING + 1), side, 2).start()
    load(order(1), 1).start()

    barrier = pltpu.get_barrier_semaphore()

    def other_chip(step):
        return wrap(chip + step, chips)

    def other_row(step):
        return wrap(r + step, count)

    def to_chip(step):
        return {"rows": other_chip(step) * 2 + core, "snaps": z}

    def to_row(step):
        return {"rows": other_row(step), "snaps": z}

    def to_depth(step):
        return {"rows": r, "snaps": at(step)}

    @pl.loop(1, count)
    def _(step):
        pl.semaphore_signal(barrier, inc=1, device_id=to_row(step), device_id_type=MESH)

    @pl.loop(1, RING)
    def _(step):
        pl.semaphore_signal(barrier, inc=1, device_id=to_depth(step), device_id_type=MESH)

    def ring(side, src, dst, send, recv):
        return pltpu.make_async_remote_copy(
            src_ref=src,
            dst_ref=dst,
            send_sem=send,
            recv_sem=recv,
            device_id={"rows": r, "snaps": at(1 - 2 * side)},
            device_id_type=MESH,
        )

    def span_of(i):
        return pl.ds(0, size + 16) if i == 0 else pl.ds(size + 16, size)

    def data_of(i):
        return pl.ds(0, size) if i == 0 else pl.ds(size + 16, size)

    scale_rows = pl.ds(size, 16)

    def sum_copy(side, u, i):
        return ring(
            side,
            tx.at[side, u, span_of(i), :],
            rx.at[side, u, span_of(i), :],
            rs_send.at[side],
            rs_recv.at[side, 2 * u + i],
        )

    def piece(q):
        return pl.ds(pl.multiple_of(q * size, size), size)

    def sketch(slot):
        if slot + 2 < RING:
            load(order(slot + 2), slot + 2).start()
        load(order(slot), slot).wait()
        j = at(order(slot))
        rows = pl.ds(pl.multiple_of(j * shard, shard), shard)
        part[j] = jnp.dot(s[rows, :], k[...], preferred_element_type=F32)

    def pair_rows(j, side, u):
        first = 2 * size * (u % 2 if side == 0 else 1 - u % 2)
        return j, pl.ds(pl.multiple_of(first, 2 * size), 2 * size)

    def piece_rows(j, side, u, i):
        first = 2 * size * (u % 2 if side == 0 else 1 - u % 2) + i * size
        return j, pl.ds(pl.multiple_of(first, size), size)

    def set_scale(side, u, top):
        tx[side, u, scale_rows, :] = (top * 1.01 + 1e-30).astype(BF16)

    def send(side, u, i, value):
        tx[side, u, data_of(i), :] = encode(value, tx[side, u, scale_rows, :])
        sum_copy(side, u, i).start()

    def came(side, u, i):
        return decode(rx[side, u, data_of(i), :], rx[side, u, scale_rows, :])

    def head(side, u, offset):
        j = at(offset)
        set_scale(side, u, peak(part[pair_rows(j, side, u)]))
        for i in range(2):
            send(side, u, i, part[piece_rows(j, side, u, i)])

    sketch_copy.wait()
    load(order(2), 2).start()
    for side in range(2):
        load(order(0), side * (RING + 1), side, 2).wait()
        first = side * 2 * size
        rows = pl.ds(pl.multiple_of(at(order(0)) * shard + first, 2 * size), 2 * size)
        part[at(order(0)), pl.ds(first, 2 * size), :] = jnp.dot(s[rows, :], k[...], preferred_element_type=F32)
        if side == 0:
            pl.semaphore_wait(barrier, count - 1 + RING - 1)
        head(side, 0, 4)
    for side in range(2):
        sketch(1 + side)
        head(side, 1, 3 - 6 * side)
    for slot in range(3, RING):
        sketch(slot)

    @pl.loop(0, RING - 3)
    def _(u):
        far = 4 - (u + 1) // 2
        for i in range(2):
            for side in range(2):
                j = at((1 - 2 * side) * (far - 1))
                sum_copy(side, u, i).wait_recv()
                if i == 0:
                    set_scale(side, u + 2, rx[side, u, scale_rows, :].astype(F32) + peak(part[pair_rows(j, side, u)]))
                send(side, u + 2, i, part[piece_rows(j, side, u, i)] + came(side, u, i))

    def gather_copy(side, e, j, q):
        block = everyone.at[j, piece(q), :]
        return ring(side, block, block, ag_send, ag_recv.at[side, e])

    def gather_piece(side, e):
        hop = jnp.minimum(e // 4 + 1, 4)
        i = jnp.where(e < 12, e % 4, 2 * (e - 12))
        odd = i % 2
        return hop, 2 * (odd if side == 0 else 1 - odd) + i // 2

    def gram(pieces):
        rows = jnp.concatenate([part[z, piece(q), :] for q in pieces], axis=0)
        both = jnp.concatenate(split(rows), axis=1)
        gg[...] += lax.dot_general(both, both, (((0,), (0,)), ((), ())), preferred_element_type=F32)

    gg[...] = jnp.zeros_like(gg)
    for i in range(2):
        for side in range(2):
            sum_copy(side, RING - 3, i).wait_recv()
            part[piece_rows(z, side, RING - 3, i)] += came(side, RING - 3, i)
    for i in range(2):
        for side in range(2):
            sum_copy(side, RING - 2, i).wait_recv()
            mine = part[piece_rows(z, side, RING - 2, i)] + came(side, RING - 2, i)
            part[piece_rows(z, side, RING - 2, i)] = mine
            everyone[piece_rows(z, side, RING - 2, i)] = mine.astype(BF16)
        for side in range(2):
            for odd in range(2):
                e = 2 * i + odd
                gather_copy(side, e, z, gather_piece(side, e)[1]).start()
        gram((i, 2 + i))

    g[...] = gg[:rank, :rank] + gg[:rank, rank:] + gg[rank:, :rank] + gg[rank:, rank:]
    for index in range(count):
        g0[index] = g[index * half : (index + 1) * half, :]

    def remote(src, dst, send_sem, recv_sem, there):
        return pltpu.make_async_remote_copy(
            src_ref=src,
            dst_ref=dst,
            send_sem=send_sem,
            recv_sem=recv_sem,
            device_id=there,
            device_id_type=MESH,
        )

    def g1_copy(step):
        return remote(g0.at[other_row(step)], g1.at[step], g1_sem.at[0], g1_sem.at[1], to_row(step))

    def g2_copy(step):
        return remote(g2.at[z], g2.at[z], g2_sem.at[0], g2_sem.at[1], to_depth(step))

    def g3_copy(step):
        return remote(g3.at[r], g3.at[r], g3_sem.at[0], g3_sem.at[1], to_row(step))

    def zr_copy(step):
        return remote(pair.at[other_chip(step)], zr.at[step], zr_sem.at[0], zr_sem.at[1], to_chip(step))

    def all_of(ref, number, sem):
        block = ref.at[pl.ds(0, number)]
        return remote(block, block, sem.at[0], sem.at[1], to_row(1))

    def start_all(copy, number):
        for step in range(1, number):
            copy(step).start()

    start_all(g1_copy, count)

    def term_of(pairs):
        left = [everyone[j, piece(q), :] for j, q in pairs]
        right = [s[pl.ds(pl.multiple_of(j * shard + q * size, size), size), :] for j, q in pairs]
        return lax.dot_general(
            jnp.concatenate(left, axis=0),
            jnp.concatenate(right, axis=0),
            (((0,), (0,)), ((), ())),
            preferred_element_type=F32,
        )

    def gather(e):
        came = []
        for side in range(2):
            hop, q = gather_piece(side, e)
            j = at(-(1 - 2 * side) * hop)
            came.append((j, q))
            gather_copy(side, e, j, q).wait_recv()

            @pl.when((e < 8) | (e == 8) | (e == 10))
            def _():
                gather_copy(side, jnp.where(e < 8, e + 4, 12 + (e - 8) // 2), j, q).start()

        z_sum[...] += term_of(came)

    z_sum[...] = term_of([(z, q) for q in range(PIECES)])
    gather(0)
    all_of(g1, count - 1, g1_sem).wait_recv()
    g1[0] = g0[r]
    g2[z] = jnp.sum(g1[...], axis=0)
    start_all(g2_copy, RING)

    @pl.loop(1, 3)
    def _(e):
        gather(e)

    all_of(g2, RING - 1, g2_sem).wait_recv()
    g3[r] = jnp.sum(g2[...], axis=0) * (1.0 / total)
    start_all(g3_copy, count)
    gather(3)
    all_of(g3, count - 1, g3_sem).wait_recv()
    for index in range(count):
        g[index * half : (index + 1) * half, :] = g3[index]

    eye = lax.broadcasted_iota(jnp.int32, (rank, rank), 0) == lax.broadcasted_iota(jnp.int32, (rank, rank), 1)
    full = g[...]
    diagonal = jnp.where(eye, full, 0.0)
    down = lax.rsqrt(jnp.sum(diagonal, axis=1, keepdims=True))
    across = lax.rsqrt(jnp.sum(diagonal, axis=0, keepdims=True))
    x[...] = jnp.concatenate([full * down * across, jnp.where(eye, down, 0.0)], axis=1)

    @pl.loop(4, EVENTS - 2)
    def _(e):
        gather(e)
        factor_block(x, e - 4)

    @pl.loop(EVENTS - 2, EVENTS)
    def _(e):
        gather(e)

    l1, l2 = split(x[:, rank:])
    z1, z2 = split(z_sum[...])
    term = jnp.dot(
        jnp.concatenate([l1, l2, l1], axis=1),
        jnp.concatenate([z1, z1, z2], axis=0),
        preferred_element_type=F32,
    ) * (1.0 / math.sqrt(total))
    z_sum[...] = term
    for c in range(chips):
        rows = z_sum[c * own : (c + 1) * own, :]
        low, high = rows[:half], rows[half:]
        give[c] = jnp.where(core == 0, high, low)
        pair[c] = jnp.where(core == 0, low, high)
    mate = remote(give, take, mate_send, mate_recv, {"rows": chip * 2 + 1 - core, "snaps": z})
    mate.start()
    i1, i2 = split(x[:, rank:])
    mate.wait_recv()
    pair[...] += take[...]

    start_all(zr_copy, chips)

    @pl.loop(0, PIECES)
    def _(q):
        y1, y2 = split(part[z, piece(q), :])
        basis_ref[piece(q), :] = lax.dot_general(
            jnp.concatenate([y1, y1, y2], axis=1),
            jnp.concatenate([i1, i2, i1], axis=1),
            (((1,), (1,)), ((), ())),
            preferred_element_type=F32,
        )

    mate.wait_send()

    for side in range(2):
        ring(side, tx.at[side], tx.at[side], rs_send.at[side], rs_recv.at[side, 0]).wait_send()
    sent = everyone.at[pl.ds(0, RING - 1)]
    ring(0, sent, sent, ag_send, ag_recv.at[0, 0]).wait_send()
    all_of(g1, count - 1, g1_sem).wait_send()
    all_of(g2, RING - 1, g2_sem).wait_send()
    all_of(g3, count - 1, g3_sem).wait_send()

    all_of(zr, chips - 1, zr_sem).wait_recv()
    zr[0] = pair[chip]
    proj_ref[...] = jnp.sum(zr[...], axis=0)
    all_of(zr, chips - 1, zr_sem).wait_send()


def finish(basis_in, proj_in, basis_out, proj_out, sem):
    copies = [pltpu.make_async_copy(proj_in, proj_out, sem.at[0])]
    size = basis_in.shape[0] // PIECES
    for q in range(PIECES):
        rows = pl.ds(q * size, size)
        copies.append(pltpu.make_async_copy(basis_in.at[rows, :], basis_out.at[rows, :], sem.at[1 + q]))
    for copy in copies:
        copy.start()
    for copy in copies:
        copy.wait()


def local(snapshots, sketch):
    rows, columns = snapshots.shape
    rank = sketch.shape[1]
    count = lax.axis_size("rows")
    chips = count // 2
    total = rows * count
    shard = rows // RING
    half = rank // count
    message = 2 * (shard // PIECES) + 16
    dma = pltpu.SemaphoreType.DMA
    outputs = (
        jax.ShapeDtypeStruct((shard, rank), F32),
        jax.ShapeDtypeStruct((half, columns), F32),
    )
    anywhere = pl.BlockSpec(memory_space=pl.ANY)
    basis, projected = pl.pallas_call(
        functools.partial(kernel, total),
        out_shape=tuple(pltpu.VMEM(out.shape, out.dtype) for out in outputs),
        in_specs=[anywhere] * 2,
        out_specs=(pl.BlockSpec(memory_space=pltpu.VMEM),) * 2,
        scratch_shapes=[
            pltpu.VMEM((rows, columns), BF16),
            pltpu.VMEM((columns, rank), BF16),
            pltpu.VMEM((RING, shard, rank), F32),
            pltpu.VMEM((2, RING - 1, message, rank), BF16),
            pltpu.VMEM((2, RING - 1, message, rank), BF16),
            pltpu.VMEM((RING, shard, rank), BF16),
            pltpu.VMEM((rank, columns), F32),
            pltpu.VMEM((2 * rank, 2 * rank), F32),
            pltpu.VMEM((rank, rank), F32),
            pltpu.VMEM((count, half, rank), F32),
            pltpu.VMEM((count, half, rank), F32),
            pltpu.VMEM((RING, half, rank), F32),
            pltpu.VMEM((count, half, rank), F32),
            pltpu.VMEM((rank, 2 * rank), F32),
            pltpu.VMEM((chips, half, columns), F32),
            pltpu.VMEM((chips, half, columns), F32),
            pltpu.VMEM((chips, half, columns), F32),
            pltpu.VMEM((chips, half, columns), F32),
            dma((RING + 2,)),
            dma((2,)),
            dma((2, EVENTS)),
            dma,
            dma((2, EVENTS)),
            dma((2,)),
            dma((2,)),
            dma((2,)),
            dma((2,)),
            dma,
            dma,
        ],
        compiler_params=pltpu.CompilerParams(
            collective_id=0, has_side_effects=True, vmem_limit_bytes=56 * 1024 * 1024
        ),
    )(snapshots, sketch)
    return pl.pallas_call(
        finish,
        out_shape=outputs,
        in_specs=[pl.BlockSpec(memory_space=pltpu.VMEM)] * 2,
        out_specs=(anywhere, anywhere),
        scratch_shapes=[dma((PIECES + 1,))],
        compiler_params=pltpu.CompilerParams(vmem_limit_bytes=16 * 1024 * 1024),
    )(basis, projected)


def solution(mesh):
    in_specs = (P("rows", "snaps"), P("snaps", None))
    out_specs = (P(("rows", "snaps"), None), P("rows", "snaps"))
    return jax.shard_map(local, mesh=mesh, in_specs=in_specs, out_specs=out_specs, check_vma=False)
```

time: 71.2 us -> 69.4 us (0.975)
  Pallas kernels: 70.4 us -> 68.6 us
    pallas_call x2, Pallas kernels: 70.4 us -> 68.6 us  [the longest x1 67.8 us: local(): pl.pallas_call(functools.partial(kernel, total), out_shape=tuple((pltpu.V...]
where the time goes in v4:
time: 69.4 us; the launch traced here: 69.2 us
  Pallas kernels  68.6 us (99%)
    pallas_call x1, Pallas kernels, local(): pl.pallas_call(functools.partial(kernel, total), out_shape=tuple((pltpu.V...  67.8 us

profile of v4, /device:TPU:1, one launch (start us, length us, event | category | flops | bytes accessed | tf_op | source)
XLA Modules:
  0.0 69.2 jit_solution(15974672875554024899)
XLA Ops:
  0.6 67.8 %shard_map.41 = (f32[1024,128]{1,0:T(8,128)S(1)}, f32[4,512]{1,0:T(4,128)S(1)}) custom-call(bf16[8192,512]{1,0:T(8,128)(2,1)} %s_hbm.1, bf16[512,128]{1,0:T(8,128)(2,1)} %k_hbm.1), custom_call_target="tpu_custom_call" | custom-call | tf_op jit(solution)/shard_map/pallas_call | solution.py:448
  68.4 0.8 %shard_map.42 = (f32[1024,128]{1,0:T(8,128)}, f32[4,512]{1,0:T(4,128)}) custom-call(f32[1024,128]{1,0:T(8,128)S(1)} %get-tuple-element.4.basis_in, f32[4,512]{1,0:T(4,128)S(1)} %get-tuple-element.5.proj_in), custom_call_target="tpu_custom_call" | custom-call | tf_op jit(solution)/shard_map/pallas_call | solution.py:488

commit v5 on v4

--- a/solution.py
+++ b/solution.py
@@ -113,8 +113,10 @@
         index = jnp.where(index >= length, index - length, index)
         return jnp.where(index < 0, index + length, index)
 
+    sense = 1 - 2 * core
+
     def at(step):
-        return wrap(z + step, RING)
+        return wrap(z + sense * step, RING)
 
     def load(offset, slot, part_of=0, parts=1):
         length = shard // parts
@@ -147,13 +149,8 @@
     def to_depth(step):
         return {"rows": r, "snaps": at(step)}
 
-    @pl.loop(1, count)
-    def _(step):
-        pl.semaphore_signal(barrier, inc=1, device_id=to_row(step), device_id_type=MESH)
-
-    @pl.loop(1, RING)
-    def _(step):
-        pl.semaphore_signal(barrier, inc=1, device_id=to_depth(step), device_id_type=MESH)
+    for there in [to_depth(step) for step in range(1, RING)] + [to_row(step) for step in range(1, count)]:
+        pl.semaphore_signal(barrier, inc=1, device_id=there, device_id_type=MESH)
 
     def ring(side, src, dst, send, recv):
         return pltpu.make_async_remote_copy(

time: 69.4 us -> 69.5 us (level)
  no operation moved by 1% of the time
where the time goes in v5:
time: 69.5 us; the launch traced here: 69.4 us
  Pallas kernels  68.8 us (99%)
    pallas_call x1, Pallas kernels, local(): pl.pallas_call(functools.partial(kernel, total), out_shape=tuple((pltpu.V...  67.9 us

profile of v5, /device:TPU:1, one launch (start us, length us, event | category | flops | bytes accessed | tf_op | source)
XLA Modules:
  0.0 69.4 jit_solution(3672410612166895658)
XLA Ops:
  0.6 67.9 %shard_map.41 = (f32[1024,128]{1,0:T(8,128)S(1)}, f32[4,512]{1,0:T(4,128)S(1)}) custom-call(bf16[8192,512]{1,0:T(8,128)(2,1)} %s_hbm.1, bf16[512,128]{1,0:T(8,128)(2,1)} %k_hbm.1), custom_call_target="tpu_custom_call" | custom-call | tf_op jit(solution)/shard_map/pallas_call | solution.py:445
  68.6 0.8 %shard_map.42 = (f32[1024,128]{1,0:T(8,128)}, f32[4,512]{1,0:T(4,128)}) custom-call(f32[1024,128]{1,0:T(8,128)S(1)} %get-tuple-element.4.basis_in, f32[4,512]{1,0:T(4,128)S(1)} %get-tuple-element.5.proj_in), custom_call_target="tpu_custom_call" | custom-call | tf_op jit(solution)/shard_map/pallas_call | solution.py:485

commit v6 on v4

--- a/solution.py
+++ b/solution.py
@@ -204,8 +204,11 @@
     def set_scale(side, u, top):
         tx[side, u, scale_rows, :] = (top * 1.01 + 1e-30).astype(BF16)
 
+    def set_data(side, u, i, value):
+        tx[side, u, data_of(i), :] = encode(value, tx[side, u, scale_rows, :])
+
     def send(side, u, i, value):
-        tx[side, u, data_of(i), :] = encode(value, tx[side, u, scale_rows, :])
+        set_data(side, u, i, value)
         sum_copy(side, u, i).start()
 
     def came(side, u, i):
@@ -224,9 +227,14 @@
         first = side * 2 * size
         rows = pl.ds(pl.multiple_of(at(order(0)) * shard + first, 2 * size), 2 * size)
         part[at(order(0)), pl.ds(first, 2 * size), :] = jnp.dot(s[rows, :], k[...], preferred_element_type=F32)
+        j = at(4)
+        set_scale(side, 0, peak(part[pair_rows(j, side, 0)]))
+        for i in range(2):
+            set_data(side, 0, i, part[piece_rows(j, side, 0, i)])
         if side == 0:
             pl.semaphore_wait(barrier, count - 1 + RING - 1)
-        head(side, 0, 4)
+        for i in range(2):
+            sum_copy(side, 0, i).start()
     for side in range(2):
         sketch(1 + side)
         head(side, 1, 3 - 6 * side)
@@ -253,6 +261,12 @@
         i = jnp.where(e < 12, e % 4, 2 * (e - 12))
         odd = i % 2
         return hop, 2 * (odd if side == 0 else 1 - odd) + i // 2
+
+    def start_own(i):
+        for side in range(2):
+            for odd in range(2):
+                e = 2 * i + odd
+                gather_copy(side, e, z, gather_piece(side, e)[1]).start()
 
     def gram(pieces):
         rows = jnp.concatenate([part[z, piece(q), :] for q in pieces], axis=0)
@@ -270,10 +284,8 @@
             mine = part[piece_rows(z, side, RING - 2, i)] + came(side, RING - 2, i)
             part[piece_rows(z, side, RING - 2, i)] = mine
             everyone[piece_rows(z, side, RING - 2, i)] = mine.astype(BF16)
-        for side in range(2):
-            for odd in range(2):
-                e = 2 * i + odd
-                gather_copy(side, e, z, gather_piece(side, e)[1]).start()
+        if i == 0:
+            start_own(0)
         gram((i, 2 + i))
 
     g[...] = gg[:rank, :rank] + gg[:rank, rank:] + gg[rank:, :rank] + gg[rank:, rank:]
@@ -311,6 +323,7 @@
             copy(step).start()
 
     start_all(g1_copy, count)
+    start_own(1)
 
     def term_of(pairs):
         left = [everyone[j, piece(q), :] for j, q in pairs]
@@ -334,23 +347,26 @@
             def _():
                 gather_copy(side, jnp.where(e < 8, e + 4, 12 + (e - 8) // 2), j, q).start()
 
-        z_sum[...] += term_of(came)
+        return term_of(came)
 
     z_sum[...] = term_of([(z, q) for q in range(PIECES)])
-    gather(0)
     all_of(g1, count - 1, g1_sem).wait_recv()
     g1[0] = g0[r]
     g2[z] = jnp.sum(g1[...], axis=0)
     start_all(g2_copy, RING)
 
-    @pl.loop(1, 3)
+    @pl.loop(0, 2)
     def _(e):
-        gather(e)
+        z_sum[...] += gather(e)
 
     all_of(g2, RING - 1, g2_sem).wait_recv()
     g3[r] = jnp.sum(g2[...], axis=0) * (1.0 / total)
     start_all(g3_copy, count)
-    gather(3)
+
+    @pl.loop(2, 4)
+    def _(e):
+        z_sum[...] += gather(e)
+
     all_of(g3, count - 1, g3_sem).wait_recv()
     for index in range(count):
         g[index * half : (index + 1) * half, :] = g3[index]
@@ -364,15 +380,13 @@
 
     @pl.loop(4, EVENTS - 2)
     def _(e):
-        gather(e)
+        z_sum[...] += gather(e)
         factor_block(x, e - 4)
 
-    @pl.loop(EVENTS - 2, EVENTS)
-    def _(e):
-        gather(e)
+    z_sum[...] += gather(EVENTS - 2)
 
     l1, l2 = split(x[:, rank:])
-    z1, z2 = split(z_sum[...])
+    z1, z2 = split(z_sum[...] + gather(EVENTS - 1))
     term = jnp.dot(
         jnp.concatenate([l1, l2, l1], axis=1),
         jnp.concatenate([z1, z1, z2], axis=0),

time: 69.4 us -> 68.2 us (0.983)
  Pallas kernels: 68.6 us -> 67.4 us
    pallas_call x1, Pallas kernels: 67.8 us -> 66.6 us  [local(): pl.pallas_call(functools.partial(kernel, total), out_shape=tuple((pltpu.V...]
where the time goes in v6:
time: 68.2 us; the launch traced here: 68.1 us
  Pallas kernels  67.4 us (99%)
    pallas_call x1, Pallas kernels, local(): pl.pallas_call(functools.partial(kernel, total), out_shape=tuple((pltpu.V...  66.6 us

profile of v6, /device:TPU:1, one launch (start us, length us, event | category | flops | bytes accessed | tf_op | source)
XLA Modules:
  0.0 68.1 jit_solution(5590803107764930746)
XLA Ops:
  0.6 66.6 %shard_map.41 = (f32[1024,128]{1,0:T(8,128)S(1)}, f32[4,512]{1,0:T(4,128)S(1)}) custom-call(bf16[8192,512]{1,0:T(8,128)(2,1)} %s_hbm.1, bf16[512,128]{1,0:T(8,128)(2,1)} %k_hbm.1), custom_call_target="tpu_custom_call" | custom-call | tf_op jit(solution)/shard_map/pallas_call | solution.py:462
  67.2 0.8 %shard_map.42 = (f32[1024,128]{1,0:T(8,128)}, f32[4,512]{1,0:T(4,128)}) custom-call(f32[1024,128]{1,0:T(8,128)S(1)} %get-tuple-element.4.basis_in, f32[4,512]{1,0:T(4,128)S(1)} %get-tuple-element.5.proj_in), custom_call_target="tpu_custom_call" | custom-call | tf_op jit(solution)/shard_map/pallas_call | solution.py:502

commit v7 on v6

--- a/solution.py
+++ b/solution.py
@@ -127,8 +127,8 @@
     sketch_copy = pltpu.make_async_copy(k_hbm, k, load_sem.at[RING])
     sketch_copy.start()
     for side in range(2):
-        load(order(0), side * (RING + 1), side, 2).start()
-    load(order(1), 1).start()
+        load(order(0), side * (RING + 1), side, 2).start(priority=1)
+    load(order(1), 1).start(priority=1)
 
     barrier = pltpu.get_barrier_semaphore()
 
@@ -187,7 +187,7 @@
 
     def sketch(slot):
         if slot + 2 < RING:
-            load(order(slot + 2), slot + 2).start()
+            load(order(slot + 2), slot + 2).start(priority=1)
         load(order(slot), slot).wait()
         j = at(order(slot))
         rows = pl.ds(pl.multiple_of(j * shard, shard), shard)
@@ -221,7 +221,7 @@
             send(side, u, i, part[piece_rows(j, side, u, i)])
 
     sketch_copy.wait()
-    load(order(2), 2).start()
+    load(order(2), 2).start(priority=1)
     for side in range(2):
         load(order(0), side * (RING + 1), side, 2).wait()
         first = side * 2 * size

time: 68.2 us -> 68.2 us (level)
  no operation moved by 1% of the time
where the time goes in v7:
time: 68.2 us; the launch traced here: 68.1 us
  Pallas kernels  67.4 us (99%)
    pallas_call x1, Pallas kernels, local(): pl.pallas_call(functools.partial(kernel, total), out_shape=tuple((pltpu.V...  66.6 us

profile of v7, /device:TPU:1, one launch (start us, length us, event | category | flops | bytes accessed | tf_op | source)
XLA Modules:
  0.0 68.1 jit_solution(13221812683199896539)
XLA Ops:
  0.6 66.6 %shard_map.41 = (f32[1024,128]{1,0:T(8,128)S(1)}, f32[4,512]{1,0:T(4,128)S(1)}) custom-call(bf16[8192,512]{1,0:T(8,128)(2,1)} %s_hbm.1, bf16[512,128]{1,0:T(8,128)(2,1)} %k_hbm.1), custom_call_target="tpu_custom_call" | custom-call | tf_op jit(solution)/shard_map/pallas_call | solution.py:462
  67.2 0.8 %shard_map.42 = (f32[1024,128]{1,0:T(8,128)}, f32[4,512]{1,0:T(4,128)}) custom-call(f32[1024,128]{1,0:T(8,128)S(1)} %get-tuple-element.4.basis_in, f32[4,512]{1,0:T(4,128)S(1)} %get-tuple-element.5.proj_in), custom_call_target="tpu_custom_call" | custom-call | tf_op jit(solution)/shard_map/pallas_call | solution.py:502

commit v8 on v6

--- a/solution.py
+++ b/solution.py
@@ -122,12 +122,12 @@
         return pltpu.make_async_copy(s_hbm.at[rows, :], s.at[rows, :], load_sem.at[slot])
 
     def order(slot):
-        return (RING - slot) // 2 * (1 - 2 * ((slot + 1) % 2)) if slot else RING // 2
+        return (RING - slot) // 2 * (1 - 2 * ((slot + 1) % 2))
 
     sketch_copy = pltpu.make_async_copy(k_hbm, k, load_sem.at[RING])
     sketch_copy.start()
     for side in range(2):
-        load(order(0), side * (RING + 1), side, 2).start()
+        load(RING // 2, side * (RING + 1), side, 2).start()
     load(order(1), 1).start()
 
     barrier = pltpu.get_barrier_semaphore()
@@ -186,8 +186,10 @@
         return pl.ds(pl.multiple_of(q * size, size), size)
 
     def sketch(slot):
-        if slot + 2 < RING:
+        @pl.when(slot + 2 < RING)
+        def _():
             load(order(slot + 2), slot + 2).start()
+
         load(order(slot), slot).wait()
         j = at(order(slot))
         rows = pl.ds(pl.multiple_of(j * shard, shard), shard)
@@ -223,10 +225,10 @@
     sketch_copy.wait()
     load(order(2), 2).start()
     for side in range(2):
-        load(order(0), side * (RING + 1), side, 2).wait()
+        load(RING // 2, side * (RING + 1), side, 2).wait()
         first = side * 2 * size
-        rows = pl.ds(pl.multiple_of(at(order(0)) * shard + first, 2 * size), 2 * size)
-        part[at(order(0)), pl.ds(first, 2 * size), :] = jnp.dot(s[rows, :], k[...], preferred_element_type=F32)
+        rows = pl.ds(pl.multiple_of(at(RING // 2) * shard + first, 2 * size), 2 * size)
+        part[at(RING // 2), pl.ds(first, 2 * size), :] = jnp.dot(s[rows, :], k[...], preferred_element_type=F32)
         j = at(4)
         set_scale(side, 0, peak(part[pair_rows(j, side, 0)]))
         for i in range(2):
@@ -238,7 +240,8 @@
     for side in range(2):
         sketch(1 + side)
         head(side, 1, 3 - 6 * side)
-    for slot in range(3, RING):
+    @pl.loop(3, RING)
+    def _(slot):
         sketch(slot)
 
     @pl.loop(0, RING - 3)

time: 68.2 us -> 68.2 us (level)
  no operation moved by 1% of the time
where the time goes in v8:
time: 68.2 us; the launch traced here: 68.1 us
  Pallas kernels  67.4 us (99%)
    pallas_call x1, Pallas kernels, local(): pl.pallas_call(functools.partial(kernel, total), out_shape=tuple((pltpu.V...  66.6 us

profile of v8, /device:TPU:1, one launch (start us, length us, event | category | flops | bytes accessed | tf_op | source)
XLA Modules:
  0.0 68.1 jit_solution(16197222662423726814)
XLA Ops:
  0.6 66.6 %shard_map.41 = (f32[1024,128]{1,0:T(8,128)S(1)}, f32[4,512]{1,0:T(4,128)S(1)}) custom-call(bf16[8192,512]{1,0:T(8,128)(2,1)} %s_hbm.1, bf16[512,128]{1,0:T(8,128)(2,1)} %k_hbm.1), custom_call_target="tpu_custom_call" | custom-call | tf_op jit(solution)/shard_map/pallas_call | solution.py:465
  67.2 0.8 %shard_map.42 = (f32[1024,128]{1,0:T(8,128)}, f32[4,512]{1,0:T(4,128)}) custom-call(f32[1024,128]{1,0:T(8,128)S(1)} %get-tuple-element.4.basis_in, f32[4,512]{1,0:T(4,128)S(1)} %get-tuple-element.5.proj_in), custom_call_target="tpu_custom_call" | custom-call | tf_op jit(solution)/shard_map/pallas_call | solution.py:505

commit v9 on v8

--- a/solution.py
+++ b/solution.py
@@ -147,13 +147,8 @@
     def to_depth(step):
         return {"rows": r, "snaps": at(step)}
 
-    @pl.loop(1, count)
-    def _(step):
-        pl.semaphore_signal(barrier, inc=1, device_id=to_row(step), device_id_type=MESH)
-
-    @pl.loop(1, RING)
-    def _(step):
-        pl.semaphore_signal(barrier, inc=1, device_id=to_depth(step), device_id_type=MESH)
+    for there in [to_depth(step) for step in range(1, RING)] + [to_row(step) for step in range(1, count)]:
+        pl.semaphore_signal(barrier, inc=1, device_id=there, device_id_type=MESH)
 
     def ring(side, src, dst, send, recv):
         return pltpu.make_async_remote_copy(

time: 68.2 us -> 68.2 us (level)
  no operation moved by 1% of the time
where the time goes in v9:
time: 68.2 us; the launch traced here: 68.1 us
  Pallas kernels  67.4 us (99%)
    pallas_call x1, Pallas kernels, local(): pl.pallas_call(functools.partial(kernel, total), out_shape=tuple((pltpu.V...  66.6 us

profile of v9, /device:TPU:1, one launch (start us, length us, event | category | flops | bytes accessed | tf_op | source)
XLA Modules:
  0.0 68.1 jit_solution(4147213955080011023)
XLA Ops:
  0.6 66.6 %shard_map.41 = (f32[1024,128]{1,0:T(8,128)S(1)}, f32[4,512]{1,0:T(4,128)S(1)}) custom-call(bf16[8192,512]{1,0:T(8,128)(2,1)} %s_hbm.1, bf16[512,128]{1,0:T(8,128)(2,1)} %k_hbm.1), custom_call_target="tpu_custom_call" | custom-call | tf_op jit(solution)/shard_map/pallas_call | solution.py:460
  67.2 0.8 %shard_map.42 = (f32[1024,128]{1,0:T(8,128)}, f32[4,512]{1,0:T(4,128)}) custom-call(f32[1024,128]{1,0:T(8,128)S(1)} %get-tuple-element.4.basis_in, f32[4,512]{1,0:T(4,128)S(1)} %get-tuple-element.5.proj_in), custom_call_target="tpu_custom_call" | custom-call | tf_op jit(solution)/shard_map/pallas_call | solution.py:500

commit v10 on v9

--- a/solution.py
+++ b/solution.py
@@ -96,17 +96,14 @@
 
 def kernel(
     total, s_hbm, k_hbm, basis_ref, proj_ref,
-    s, k, part, tx, rx, everyone, z_sum, gg, g, g0, g1, g2, g3, x, give, take, pair, zr,
-    load_sem, rs_send, rs_recv, ag_send, ag_recv, g1_sem, g2_sem, g3_sem, zr_sem, mate_send, mate_recv,
+    s, k, part, tx, rx, everyone, z_sum, gg, g, g0, g1, g2, g3, x, pair, zr,
+    load_sem, rs_send, rs_recv, ag_send, ag_recv, g1_sem, g2_sem, g3_sem, zr_sem,
 ):
     count = lax.axis_size("rows")
-    chips = count // 2
     r, z = lax.axis_index("rows"), lax.axis_index("snaps")
-    chip, core = lax.div(r, 2), lax.rem(r, 2)
     shard = part.shape[1]
     size = shard // PIECES
     rank = k.shape[1]
-    own = rank // chips
     half = rank // count
 
     def wrap(index, length):
@@ -132,14 +129,8 @@
 
     barrier = pltpu.get_barrier_semaphore()
 
-    def other_chip(step):
-        return wrap(chip + step, chips)
-
     def other_row(step):
         return wrap(r + step, count)
-
-    def to_chip(step):
-        return {"rows": other_chip(step) * 2 + core, "snaps": z}
 
     def to_row(step):
         return {"rows": other_row(step), "snaps": z}
@@ -310,7 +301,7 @@
         return remote(g3.at[r], g3.at[r], g3_sem.at[0], g3_sem.at[1], to_row(step))
 
     def zr_copy(step):
-        return remote(pair.at[other_chip(step)], zr.at[step], zr_sem.at[0], zr_sem.at[1], to_chip(step))
+        return remote(pair.at[other_row(step)], zr.at[step], zr_sem.at[0], zr_sem.at[1], to_row(step))
 
     def all_of(ref, number, sem):
         block = ref.at[pl.ds(0, number)]
@@ -391,18 +382,10 @@
         preferred_element_type=F32,
     ) * (1.0 / math.sqrt(total))
     z_sum[...] = term
-    for c in range(chips):
-        rows = z_sum[c * own : (c + 1) * own, :]
-        low, high = rows[:half], rows[half:]
-        give[c] = jnp.where(core == 0, high, low)
-        pair[c] = jnp.where(core == 0, low, high)
-    mate = remote(give, take, mate_send, mate_recv, {"rows": chip * 2 + 1 - core, "snaps": z})
-    mate.start()
+    for index in range(count):
+        pair[index] = z_sum[index * half : (index + 1) * half, :]
+    start_all(zr_copy, count)
     i1, i2 = split(x[:, rank:])
-    mate.wait_recv()
-    pair[...] += take[...]
-
-    start_all(zr_copy, chips)
 
     @pl.loop(0, PIECES)
     def _(q):
@@ -414,8 +397,6 @@
             preferred_element_type=F32,
         )
 
-    mate.wait_send()
-
     for side in range(2):
         ring(side, tx.at[side], tx.at[side], rs_send.at[side], rs_recv.at[side, 0]).wait_send()
     sent = everyone.at[pl.ds(0, RING - 1)]
@@ -424,10 +405,10 @@
     all_of(g2, RING - 1, g2_sem).wait_send()
     all_of(g3, count - 1, g3_sem).wait_send()
 
-    all_of(zr, chips - 1, zr_sem).wait_recv()
-    zr[0] = pair[chip]
+    all_of(zr, count - 1, zr_sem).wait_recv()
+    zr[0] = pair[r]
     proj_ref[...] = jnp.sum(zr[...], axis=0)
-    all_of(zr, chips - 1, zr_sem).wait_send()
+    all_of(zr, count - 1, zr_sem).wait_send()
 
 
 def finish(basis_in, proj_in, basis_out, proj_out, sem):
@@ -446,7 +427,6 @@
     rows, columns = snapshots.shape
     rank = sketch.shape[1]
     count = lax.axis_size("rows")
-    chips = count // 2
     total = rows * count
     shard = rows // RING
     half = rank // count
@@ -477,10 +457,8 @@
             pltpu.VMEM((RING, half, rank), F32),
             pltpu.VMEM((count, half, rank), F32),
             pltpu.VMEM((rank, 2 * rank), F32),
-            pltpu.VMEM((chips, half, columns), F32),
-            pltpu.VMEM((chips, half, columns), F32),
-            pltpu.VMEM((chips, half, columns), F32),
-            pltpu.VMEM((chips, half, columns), F32),
+            pltpu.VMEM((count, half, columns), F32),
+            pltpu.VMEM((count, half, columns), F32),
             dma((RING + 2,)),
             dma((2,)),
             dma((2, EVENTS)),
@@ -490,8 +468,6 @@
             dma((2,)),
             dma((2,)),
             dma((2,)),
-            dma,
-            dma,
         ],
         compiler_params=pltpu.CompilerParams(
             collective_id=0, has_side_effects=True, vmem_limit_bytes=56 * 1024 * 1024

time: 68.2 us -> 68.1 us (level)
  no operation moved by 1% of the time
where the time goes in v10:
time: 68.1 us; the launch traced here: 68 us
  Pallas kernels  67.3 us (99%)
    pallas_call x1, Pallas kernels, local(): pl.pallas_call(functools.partial(kernel, total), out_shape=tuple((pltpu.V...  66.5 us

profile of v10, /device:TPU:1, one launch (start us, length us, event | category | flops | bytes accessed | tf_op | source)
XLA Modules:
  0.0 68.0 jit_solution(16336752745668571793)
XLA Ops:
  0.6 66.5 %shard_map.41 = (f32[1024,128]{1,0:T(8,128)S(1)}, f32[4,512]{1,0:T(4,128)S(1)}) custom-call(bf16[8192,512]{1,0:T(8,128)(2,1)} %s_hbm.1, bf16[512,128]{1,0:T(8,128)(2,1)} %k_hbm.1), custom_call_target="tpu_custom_call" | custom-call | tf_op jit(solution)/shard_map/pallas_call | solution.py:440
  67.1 0.8 %shard_map.42 = (f32[1024,128]{1,0:T(8,128)}, f32[4,512]{1,0:T(4,128)}) custom-call(f32[1024,128]{1,0:T(8,128)S(1)} %get-tuple-element.4.basis_in, f32[4,512]{1,0:T(4,128)S(1)} %get-tuple-element.5.proj_in), custom_call_target="tpu_custom_call" | custom-call | tf_op jit(solution)/shard_map/pallas_call | solution.py:476

commit v11 on v9

--- a/solution.py
+++ b/solution.py
@@ -384,7 +384,13 @@
     z_sum[...] += gather(EVENTS - 2)
 
     l1, l2 = split(x[:, rank:])
-    z1, z2 = split(z_sum[...] + gather(EVENTS - 1))
+    whole = z_sum[...]
+    for side in range(2):
+        hop, q = gather_piece(side, EVENTS - 1)
+        j = at(-(1 - 2 * side) * hop)
+        gather_copy(side, EVENTS - 1, j, q).wait_recv()
+        whole = whole + term_of([(j, q)])
+    z1, z2 = split(whole)
     term = jnp.dot(
         jnp.concatenate([l1, l2, l1], axis=1),
         jnp.concatenate([z1, z1, z2], axis=0),
@@ -402,7 +408,8 @@
     mate.wait_recv()
     pair[...] += take[...]
 
-    start_all(zr_copy, chips)
+    for step in sorted(range(1, chips), key=lambda step: -min(step // 4, 4 - step // 4) - min(step % 4, 4 - step % 4)):
+        zr_copy(step).start()
 
     @pl.loop(0, PIECES)
     def _(q):

time: 68.2 us -> 67.8 us (level)
  no operation moved by 1% of the time
where the time goes in v11:
time: 67.8 us; the launch traced here: 67.7 us
  Pallas kernels  67 us (99%)
    pallas_call x1, Pallas kernels, local(): pl.pallas_call(functools.partial(kernel, total), out_shape=tuple((pltpu.V...  66.2 us

profile of v11, /device:TPU:1, one launch (start us, length us, event | category | flops | bytes accessed | tf_op | source)
XLA Modules:
  0.0 67.7 jit_solution(11181298633066506393)
XLA Ops:
  0.6 66.2 %shard_map.41 = (f32[1024,128]{1,0:T(8,128)S(1)}, f32[4,512]{1,0:T(4,128)S(1)}) custom-call(bf16[8192,512]{1,0:T(8,128)(2,1)} %s_hbm.1, bf16[512,128]{1,0:T(8,128)(2,1)} %k_hbm.1), custom_call_target="tpu_custom_call" | custom-call | tf_op jit(solution)/shard_map/pallas_call | solution.py:467
  66.8 0.8 %shard_map.42 = (f32[1024,128]{1,0:T(8,128)}, f32[4,512]{1,0:T(4,128)}) custom-call(f32[1024,128]{1,0:T(8,128)S(1)} %get-tuple-element.4.basis_in, f32[4,512]{1,0:T(4,128)S(1)} %get-tuple-element.5.proj_in), custom_call_target="tpu_custom_call" | custom-call | tf_op jit(solution)/shard_map/pallas_call | solution.py:507
